TPU v7x, 128 devices: a whole 4x4x4 slice. The times are simulated.
128 devices in a mesh: seq: 16 (over z, x_hi, core), exp: 8 (over x_lo, y).
Axes of the slice: x: 4 (x_hi: 2, x_lo: 2; x = x_hi * 2 + x_lo), y: 4, z: 4, core: 2. Of those that a mesh axis runs over, the one named last changes fastest.
Arguments:
- residual: bfloat16 [2048, 6144], P(('seq', 'exp')), may hold values from -3 to 3
- queries: bfloat16 [2048, 6144], P('seq', 'exp'), may hold values from -6 to 6
- key_heads: bfloat16 [2048, 1024], P('seq', 'exp'), may hold values from -6 to 6
- value_heads: bfloat16 [2048, 1024], P('seq', 'exp'), may hold values from -6 to 6
- out_proj: bfloat16 [6144, 6144], P('exp', 'seq'), may hold values from -0.3125 to 0.3125
- norm_gain: float32 [6144], replicated, may hold values from 0.5 to 1.5
- gate_weight: bfloat16 [8, 8192, 6144], P('exp', 'seq'), may hold values from -0.078125 to 0.078125
- up_weight: bfloat16 [8, 8192, 6144], P('exp', 'seq'), may hold values from -0.078125 to 0.078125
- down_weight: bfloat16 [8, 8192, 6144], P('exp', 'seq'), may hold values from -0.0625 to 0.0625
- adapter_in: bfloat16 [8, 1024, 6144], P('exp', 'seq'), may hold values from -0.078125 to 0.078125
- adapter_out: bfloat16 [8, 1024, 6144], P('exp', 'seq'), may hold values from -0.1875 to 0.1875
- route_ids: int32 [2048, 2], P(('seq', 'exp')), may hold values from 0 to 7, all different within a row; in each aligned block of 16 rows (0 to 15, 16 to 31, ...) at most 5 rows name the same one
- route_gates: float32 [2048, 2], P(('seq', 'exp')), may hold values from 0.2 to 1
- adapter_mix: int32 [2048, 64], P(('seq', 'exp')), may hold values from -8 to 8
Outputs:
- mixed: bfloat16 [2048, 6144], P(('seq', 'exp'))
Inputs may be any that keep to these rules, and one draw needn't show every extreme that they name: `route_ids`: in each aligned block of 16 rows (the rows of one device) no expert is named more than 5 times, a bound that some block reaches; the two experts of a row differ.
All inputs are finite; a program needn't handle non-finite values.
Results may differ from a plain program's by a relative error of at most 0.023.
Values may be sent and summed in bfloat16 or wider, within the bound.
A program may use at most 128 MiB of HBM per device.

v0:
```python
import functools

import jax
import jax.numpy as jnp
from jax import lax
from jax.experimental import pallas as pl
from jax.experimental.pallas import tpu as pltpu
from jax.sharding import PartitionSpec as P

RANK = 16


MESH = pl.DeviceIdType.MESH
CAP = 5
Z = 4


def dot(left, right):
    return jnp.dot(left, right, preferred_element_type=jnp.float32)


def contract_last(left, right):
    return lax.dot_general(
        left, right, (((1,), (1,)), ((), ())), preferred_element_type=jnp.float32
    )


def tile_of(size, most):
    while size % most:
        most -= 128
    return most


def place_on_mesh():
    me = lax.axis_index("seq")
    core = lax.rem(me, 2)
    x_hi = lax.rem(me // 2, 2)
    z = me // 4
    return me, z, x_hi, core


def seq_of(z, x_hi, core):
    return lax.rem(z + Z, Z) * 4 + x_hi * 2 + core


def expert_kernel(
    exps,
    disp,
    hidden,
    slot_gates,
    gate_hbm,
    up_hbm,
    down_hbm,
    in_hbm,
    out_hbm,
    out,
    arrived,
    wide_slots,
    rows,
    w_first,
    w_second,
    units,
    pair_send,
    pair_recv,
    own,
    z_send,
    half_low,
    half_high,
    full_low,
    full_high,
    x_send,
    x_recv,
    back,
    back_wide,
    returned,
    returned_wide,
    weight_sems,
    disp_send,
    disp_recv,
    ring_send,
    ring_recv,
    pass_send,
    pass_recv,
    pair_send_sem,
    pair_recv_sem,
    z_send_sem,
    z_recv_sem,
    x_send_sem,
    x_recv_sem,
    back_send,
    back_recv,
    local_sem,
):
    bf16, f32 = jnp.bfloat16, jnp.float32
    width = hidden.shape[1]
    half = width // 2
    quarter = half // 2
    lanes = half // 128
    slot_rows = disp.shape[3]
    hidden_units = gate_hbm.shape[0]
    adapters = in_hbm.shape[0]
    block = 2 * exps * CAP
    many = 4 * block
    peers = 2 * exps

    me, z, x_hi, core = place_on_mesh()
    exp = lax.axis_index("exp")
    sibling = (seq_of(z, x_hi, 1 - core), exp)
    above = (seq_of(z + 1, x_hi, core), exp)
    below = (seq_of(z - 1, x_hi, core), exp)
    across = (seq_of(z, 1 - x_hi, core), exp)
    mine = core * exps + exp

    def peer(step):
        at = lax.rem(mine + step, peers)
        return at, (seq_of(z, x_hi, at // exps), lax.rem(at, exps))

    barrier = pltpu.get_barrier_semaphore()

    def greet(step, carry):
        pl.semaphore_signal(barrier, inc=1, device_id=peer(step)[1], device_id_type=MESH)
        return carry

    lax.fori_loop(1, peers, greet, 0)
    for other in (above, below, across):
        pl.semaphore_signal(barrier, inc=1, device_id=other, device_id_type=MESH)

    loads = []
    for side in range(2):
        columns = pl.ds(side * half, half)
        for source, place, start in (
            (gate_hbm, w_first, 0),
            (up_hbm, w_first, hidden_units),
            (in_hbm, w_first, 2 * hidden_units),
            (down_hbm, w_second, 0),
            (out_hbm, w_second, hidden_units),
        ):
            load = pltpu.make_async_copy(
                source.at[:, columns],
                place.at[side, pl.ds(start, source.shape[0]), :],
                weight_sems.at[len(loads)],
            )
            load.start()
            loads.append(load)

    pl.semaphore_wait(barrier, peers - 1 + 3)

    def remote(source, target, send, recv, device):
        return pltpu.make_async_remote_copy(
            src_ref=source,
            dst_ref=target,
            send_sem=send,
            recv_sem=recv,
            device_id=device,
            device_id_type=MESH,
        )

    def dispatch(step):
        at, device = peer(step)
        return remote(
            disp.at[at // exps, lax.rem(at, exps)],
            arrived.at[mine],
            disp_send.at[step],
            disp_recv.at[step],
            device,
        )

    def dispatch_start(step, carry):
        dispatch(step).start()
        return carry

    def dispatch_wait(step, carry):
        dispatch(step).wait()
        return carry

    lax.fori_loop(1, peers, dispatch_start, 0)
    keep = pltpu.make_async_copy(disp.at[core, exp], arrived.at[mine], local_sem)
    keep.start()
    keep.wait()
    lax.fori_loop(1, peers, dispatch_wait, 0)
    wide_slots[...] = arrived[...].astype(f32).reshape(block * slot_rows, 128)
    for lane in range(lanes + 1):
        rows[core, 0:block, lane * 128 : (lane + 1) * 128] = wide_slots[
            pl.ds(lane, block, stride=slot_rows), :
        ].astype(bf16)

    all_columns = pl.ds(0, half + 128)
    cut = (lanes + 2) // 2 * 128
    first_columns, last_columns = pl.ds(0, cut), pl.ds(cut, half + 128 - cut)

    def part(place, columns=all_columns):
        return rows.at[core, pl.ds(place * block, block), columns]

    started = []

    def begin(copy):
        copy.start()
        started.append(copy)
        return copy

    def hand_over(place):
        return begin(
            remote(part(place), part(place), pass_send.at[place], pass_recv.at[place], sibling)
        )

    def hop(index, source, target, device, columns=all_columns):
        return begin(
            remote(
                part(source, columns),
                part(target, columns),
                ring_send.at[index],
                ring_recv.at[index],
                device,
            )
        )

    handed = {}
    up_0 = hop(0, 0, 1, above)
    down_0 = hop(1, 0, 2, below)
    cross = hop(2, 0, 4, across)
    handed[0] = hand_over(0)
    up_0.wait_recv()
    up_1 = hop(3, 1, 3, above, first_columns)
    handed[1] = hand_over(1)
    down_0.wait_recv()
    down_1 = hop(4, 2, 3, below, last_columns)
    handed[2] = hand_over(2)
    cross.wait_recv()
    up_2 = hop(5, 4, 5, above)
    down_2 = hop(6, 4, 6, below)
    handed[4] = hand_over(4)
    up_1.wait_recv()
    down_1.wait_recv()
    handed[3] = hand_over(3)
    for load in loads:
        load.wait()

    unit_tile = tile_of(hidden_units, 256)
    mix_width = 64
    adapter_at = lax.broadcasted_iota(jnp.int32, (mix_width, adapters), 1) // RANK
    spread = (
        lax.broadcasted_iota(jnp.int32, (mix_width, adapters), 0)
        == adapter_at + me * (adapters // RANK)
    ).astype(bf16)

    def first_layer(group):
        at = pl.ds(group * many, many)

        def project(start, size):
            return contract_last(
                rows[0, at, 0:half], w_first[0, pl.ds(start, size), :]
            ) + contract_last(rows[1, at, 0:half], w_first[1, pl.ds(start, size), :])

        def tile(index, carry):
            start = pl.multiple_of(index * unit_tile, unit_tile)
            gate = project(start, unit_tile)
            upward = project(hidden_units + start, unit_tile)
            units[:, pl.ds(start, unit_tile)] = (jax.nn.silu(gate) * upward).astype(bf16)
            return carry

        lax.fori_loop(0, hidden_units // unit_tile, tile, 0)
        scales = dot(rows[0, at, half : half + mix_width], spread) / 8.0
        units[:, hidden_units : hidden_units + adapters] = (
            project(2 * hidden_units, adapters) * scales
        ).astype(bf16)

    out_tile = tile_of(quarter, 512)

    def second_layer(group, side, part_of, target):
        def tile(index, carry):
            start = pl.multiple_of(part_of * quarter + index * out_tile, 128)
            value = dot(units[...], w_second[side, :, pl.ds(start, out_tile)])
            target[group, :, pl.ds(start, out_tile)] = value.astype(target.dtype)
            return carry

        lax.fori_loop(0, quarter // out_tile, tile, 0)

    quarters = [pl.ds(0, quarter), pl.ds(quarter, quarter)]

    def swap(group, part_of):
        index = group * 2 + part_of
        return begin(
            remote(
                pair_send.at[group, :, quarters[part_of]],
                pair_recv.at[group, :, quarters[part_of]],
                pair_send_sem.at[index],
                pair_recv_sem.at[index],
                sibling,
            )
        )

    def z_copy(group, index, source, target, device):
        at = group * 6 + index
        return begin(remote(source, target, z_send_sem.at[at], z_recv_sem.at[at], device))

    def pair_sum(group, place, part_of):
        at = pl.ds(place * block, block)
        return own[group, at, quarters[part_of]] + pair_recv[
            group, at, quarters[part_of]
        ].astype(f32)

    def reduce_first(group, swapped, flows):
        swapped[0].wait_recv()
        z_send[group, 2, :, quarters[0]] = pair_sum(group, 3, 0).astype(bf16)
        flows["half_low"] = z_copy(
            group, 0, z_send.at[group, 2, :, quarters[0]], half_low.at[group], above
        )
        z_send[group, 0, :, quarters[0]] = pair_sum(group, 1, 0).astype(bf16)
        flows["high_0"] = z_copy(
            group,
            1,
            z_send.at[group, 0, :, quarters[0]],
            full_high.at[group, :, quarters[0]],
            below,
        )
        own[group, 0:block, quarters[0]] = pair_sum(group, 0, 0)
        own[group, 2 * block : 3 * block, quarters[0]] = pair_sum(group, 2, 0)

    def reduce_second(group, swapped, flows):
        swapped[1].wait_recv()
        z_send[group, 2, :, quarters[1]] = pair_sum(group, 3, 1).astype(bf16)
        flows["half_high"] = z_copy(
            group, 2, z_send.at[group, 2, :, quarters[1]], half_high.at[group], below
        )
        z_send[group, 1, :, quarters[1]] = pair_sum(group, 2, 1).astype(bf16)
        flows["low_1"] = z_copy(
            group,
            3,
            z_send.at[group, 1, :, quarters[1]],
            full_low.at[group, :, quarters[1]],
            above,
        )
        own[group, 0:block, quarters[1]] = pair_sum(group, 0, 1)
        own[group, block : 2 * block, quarters[1]] = pair_sum(group, 1, 1)

    def pass_on(group, flows):
        flows["half_low"].wait_recv()
        z_send[group, 1, :, quarters[0]] = (
            own[group, 2 * block : 3 * block, quarters[0]] + half_low[group].astype(f32)
        ).astype(bf16)
        flows["low_0"] = z_copy(
            group,
            4,
            z_send.at[group, 1, :, quarters[0]],
            full_low.at[group, :, quarters[0]],
            above,
        )
        flows["half_high"].wait_recv()
        z_send[group, 0, :, quarters[1]] = (
            own[group, block : 2 * block, quarters[1]] + half_high[group].astype(f32)
        ).astype(bf16)
        flows["high_1"] = z_copy(
            group,
            5,
            z_send.at[group, 0, :, quarters[1]],
            full_high.at[group, :, quarters[1]],
            below,
        )

    def settled(group, part_of, flows):
        flows[f"low_{part_of}"].wait_recv()
        flows[f"high_{part_of}"].wait_recv()
        return (
            own[group, 0:block, quarters[part_of]]
            + full_low[group, :, quarters[part_of]].astype(f32)
            + full_high[group, :, quarters[part_of]].astype(f32)
        )

    flows = ({}, {})
    for place in range(4):
        handed[place].wait_recv()
    first_layer(0)
    up_2.wait_recv()
    up_3 = hop(7, 5, 7, above, first_columns)
    handed[5] = hand_over(5)
    down_2.wait_recv()
    down_3 = hop(8, 6, 7, below, last_columns)
    handed[6] = hand_over(6)
    second_layer(0, 1 - core, 0, pair_send)
    swap_0 = [swap(0, 0)]
    second_layer(0, 1 - core, 1, pair_send)
    swap_0.append(swap(0, 1))
    second_layer(0, core, 0, own)
    reduce_first(0, swap_0, flows[0])
    second_layer(0, core, 1, own)
    reduce_second(0, swap_0, flows[0])
    up_3.wait_recv()
    down_3.wait_recv()
    handed[7] = hand_over(7)
    for place in range(4, 8):
        handed[place].wait_recv()
    first_layer(1)
    pass_on(0, flows[0])
    second_layer(1, 1 - core, 0, pair_send)
    swap_1 = [swap(1, 0)]
    second_layer(1, 1 - core, 1, pair_send)
    swap_1.append(swap(1, 1))
    second_layer(1, core, 0, own)
    reduce_first(1, swap_1, flows[1])
    second_layer(1, core, 1, own)
    reduce_second(1, swap_1, flows[1])
    pass_on(1, flows[1])
    crossing = []
    for part_of in range(2):
        own[0, 0:block, quarters[part_of]] = settled(0, part_of, flows[0])
    for part_of in (1, 0):
        x_send[:, quarters[part_of]] = settled(1, part_of, flows[1]).astype(bf16)
        crossing.append(
            begin(
                remote(
                    x_send.at[:, quarters[part_of]],
                    x_recv.at[:, quarters[part_of]],
                    x_send_sem.at[part_of],
                    x_recv_sem.at[part_of],
                    across,
                )
            )
        )
    for copy in crossing:
        copy.wait_recv()
    for lane in range(lanes):
        columns = slice(lane * 128, (lane + 1) * 128)
        back_wide[pl.ds(lane, block, stride=lanes), :] = own[0, 0:block, columns] + x_recv[
            :, columns
        ].astype(f32)
    back[...] = back_wide[...].reshape(back.shape).astype(bf16)

    def give_back(step):
        at, device = peer(step)
        return remote(
            back.at[at], returned.at[core, exp], back_send.at[step], back_recv.at[step], device
        )

    def give_start(step, carry):
        give_back(step).start()
        return carry

    def give_wait(step, carry):
        give_back(step).wait()
        return carry

    lax.fori_loop(1, peers, give_start, 0)
    keep = pltpu.make_async_copy(back.at[mine], returned.at[core, exp], local_sem)
    keep.start()
    keep.wait()
    for copy in started:
        copy.wait_send()
    lax.fori_loop(1, peers, give_wait, 0)

    slots = exps * CAP
    returned_wide[...] = returned[...].astype(f32).reshape(2 * slots * lanes, 128)
    gates = slot_gates[...]
    for side in range(2):
        for lane in range(lanes):
            columns = slice(side * half + lane * 128, side * half + (lane + 1) * 128)
            values = returned_wide[pl.ds(side * slots * lanes + lane, slots, stride=lanes), :]
            routed = jnp.dot(
                gates, values, precision=lax.Precision.HIGHEST, preferred_element_type=f32
            )
            out[:, columns] = (hidden[:, columns].astype(f32) + routed).astype(bf16)


def expert_layer(disp, hidden, slot_gates, gate, up, down, adapter_in, adapter_out):
    bf16, f32 = jnp.bfloat16, jnp.float32
    exps = disp.shape[1]
    tokens, width = hidden.shape
    half = width // 2
    lanes = half // 128
    slot_rows = disp.shape[3]
    block = 2 * exps * CAP
    hidden_units, adapters = gate.shape[0], adapter_in.shape[0]
    inner = hidden_units + adapters
    dma = pltpu.SemaphoreType.DMA
    vmem = pl.BlockSpec(memory_space=pltpu.VMEM)
    anywhere = pl.BlockSpec(memory_space=pl.ANY)
    return pl.pallas_call(
        functools.partial(expert_kernel, exps),
        out_shape=jax.ShapeDtypeStruct((tokens, width), bf16),
        in_specs=[vmem] * 3 + [anywhere] * 5,
        out_specs=vmem,
        scratch_shapes=[
            pltpu.VMEM((2 * exps, CAP, slot_rows, 128), bf16),
            pltpu.VMEM((block * slot_rows, 128), f32),
            pltpu.VMEM((2, 8 * block, half + 128), bf16),
            pltpu.VMEM((2, hidden_units + inner, half), bf16),
            pltpu.VMEM((2, inner, half), bf16),
            pltpu.VMEM((4 * block, inner), bf16),
            pltpu.VMEM((2, 4 * block, half), bf16),
            pltpu.VMEM((2, 4 * block, half), bf16),
            pltpu.VMEM((2, 4 * block, half), f32),
            pltpu.VMEM((2, 3, block, half), bf16),
            pltpu.VMEM((2, block, half // 2), bf16),
            pltpu.VMEM((2, block, half // 2), bf16),
            pltpu.VMEM((2, block, half), bf16),
            pltpu.VMEM((2, block, half), bf16),
            pltpu.VMEM((block, half), bf16),
            pltpu.VMEM((block, half), bf16),
            pltpu.VMEM((2 * exps, CAP, lanes, 128), bf16),
            pltpu.VMEM((block * lanes, 128), f32),
            pltpu.VMEM((2, exps, CAP, lanes, 128), bf16),
            pltpu.VMEM((2 * exps * CAP * lanes, 128), f32),
            dma((10,)),
            dma((2 * exps,)),
            dma((2 * exps,)),
            dma((9,)),
            dma((9,)),
            dma((8,)),
            dma((8,)),
            dma((4,)),
            dma((4,)),
            dma((12,)),
            dma((12,)),
            dma((2,)),
            dma((2,)),
            dma((2 * exps,)),
            dma((2 * exps,)),
            dma,
        ],
        compiler_params=pltpu.CompilerParams(
            collective_id=1, has_side_effects=True, vmem_limit_bytes=62 * 2**20
        ),
    )(disp, hidden, slot_gates, gate, up, down, adapter_in, adapter_out)


def attention_kernel(
    exps,
    queries,
    key_heads,
    value_heads,
    out_proj,
    residual,
    out,
    pairs,
    weights,
    attended,
    part_send,
    part_recv,
    proj_send,
    proj,
    kv_send,
    kv_recv,
    pass_send,
    pass_recv,
    w_send,
    w_recv,
    att_send,
    att_recv,
    part_send_sem,
    part_recv_sem,
    proj_send_sem,
    proj_recv_sem,
    local_sem,
):
    bf16, f32 = jnp.bfloat16, jnp.float32
    seq_rows = queries.shape[0]
    head_width = key_heads.shape[1]
    heads = queries.shape[1] // head_width
    tokens = seq_rows // exps
    columns = out_proj.shape[1]
    length = 16 * seq_rows

    me, z, x_hi, core = place_on_mesh()
    exp = lax.axis_index("exp")
    chip = z * 2 + x_hi
    sibling = (seq_of(z, x_hi, 1 - core), exp)
    across = (seq_of(z, 1 - x_hi, core), exp)

    def chip_peer(step):
        return lax.rem(chip + step, 8) * 2 + core, exp

    def z_peer(step):
        return seq_of(z + step, x_hi, core), exp

    def exp_peer(step):
        return me, lax.rem(exp + step, exps)

    barrier = pltpu.get_barrier_semaphore()

    def greet_chip(step, carry):
        pl.semaphore_signal(barrier, inc=1, device_id=chip_peer(step), device_id_type=MESH)
        return carry

    def greet_exp(step, carry):
        pl.semaphore_signal(barrier, inc=1, device_id=exp_peer(step), device_id_type=MESH)
        return carry

    lax.fori_loop(1, 8, greet_chip, 0)
    lax.fori_loop(1, exps, greet_exp, 0)
    pl.semaphore_signal(barrier, inc=1, device_id=sibling, device_id_type=MESH)
    pairs[me, :, 0:head_width] = key_heads[...]
    pairs[me, :, head_width : 2 * head_width] = value_heads[...]
    pl.semaphore_wait(barrier, 7 + exps - 1 + 1)

    def remote(source, target, send, recv, device):
        return pltpu.make_async_remote_copy(
            src_ref=source,
            dst_ref=target,
            send_sem=send,
            recv_sem=recv,
            device_id=device,
            device_id_type=MESH,
        )

    def kv_copy(step):
        return remote(
            pairs.at[me], pairs.at[me], kv_send.at[step], kv_recv.at[step], chip_peer(step)
        )

    def kv_pass(step):
        at = lax.rem(chip - step + 8, 8) * 2 + core
        return remote(pairs.at[at], pairs.at[at], pass_send.at[step], pass_recv.at[step], sibling)

    def kv_start(step, carry):
        kv_copy(step).start()
        return carry

    def kv_forward(step, carry):
        kv_copy(step).wait_recv()
        kv_pass(step).start()
        return carry

    lax.fori_loop(1, 8, kv_start, 0)
    kv_pass(0).start()

    mine = x_hi * 2 + core
    other = (1 - x_hi) * 2 + core
    w_pair = remote(out_proj, weights.at[mine], w_send.at[0], w_recv.at[0], sibling)
    w_across = remote(out_proj, weights.at[mine], w_send.at[1], w_recv.at[1], across)
    w_pass = remote(weights.at[other], weights.at[other], w_send.at[2], w_recv.at[2], sibling)
    w_keep = pltpu.make_async_copy(out_proj, weights.at[mine], local_sem)
    w_across.start()
    w_pair.start()
    w_keep.start()

    lax.fori_loop(1, 8, kv_forward, 0)

    def kv_arrive(step, carry):
        kv_pass(step).wait_recv()
        return carry

    lax.fori_loop(0, 8, kv_arrive, 0)

    scaling = head_width ** (-0.5)
    allowed = lax.broadcasted_iota(jnp.int32, (seq_rows, length), 1) <= (
        lax.broadcasted_iota(jnp.int32, (seq_rows, length), 0) + me * seq_rows
    )

    def att_copy(head, step):
        at = attended.at[z, :, pl.ds(pl.multiple_of(head * head_width, 128), head_width)]
        index = (step - 1) * heads + head
        return remote(at, at, att_send.at[index], att_recv.at[index], z_peer(step))

    def one_head(head, carry):
        span = pl.ds(pl.multiple_of(head * head_width, 128), head_width)
        all_keys = pairs[:, :, 0:head_width].reshape(length, head_width)
        scores = contract_last(queries[:, span], all_keys) * scaling
        scores = jnp.where(allowed, scores, -1e30)
        highest = jnp.max(scores, axis=1, keepdims=True)
        probs = jnp.exp(scores - highest)
        totals = jnp.sum(probs, axis=1, keepdims=True)
        all_values = pairs[:, :, head_width : 2 * head_width].reshape(length, head_width)
        summed = dot(probs.astype(bf16), all_values)
        attended[z, :, span] = (summed / totals).astype(bf16)
        for step in range(1, Z):
            att_copy(head, step).start()
        return carry

    lax.fori_loop(0, heads, one_head, 0)

    w_across.wait_recv()
    w_pass.start()
    w_keep.wait()
    w_pair.wait_recv()
    w_pass.wait_recv()

    def att_arrive(head, carry):
        for step in range(1, Z):
            att_copy(head, step).wait_recv()
        return carry

    lax.fori_loop(0, heads, att_arrive, 0)

    def part_copy(chunk, step):
        to = lax.rem(exp + step, exps)
        span = pl.ds(chunk * 2 * columns, 2 * columns)
        index = chunk * exps + step
        return remote(
            part_send.at[to, :, span],
            part_recv.at[exp, :, span],
            part_send_sem.at[index],
            part_recv_sem.at[index],
            exp_peer(step),
        )

    for chunk in range(2):
        for piece in range(2):
            block = chunk * 2 + piece
            rows = attended[...].reshape(Z * seq_rows, heads * head_width)
            value = dot(rows, weights[block]).astype(bf16)
            for z_to in range(Z):
                for exp_to in range(exps):
                    start = z_to * seq_rows + exp_to * tokens
                    part_send[
                        exp_to,
                        z_to * tokens : (z_to + 1) * tokens,
                        block * columns : (block + 1) * columns,
                    ] = value[start : start + tokens]

        def part_start(step, carry, chunk=chunk):
            part_copy(chunk, step).start()
            return carry

        lax.fori_loop(1, exps, part_start, 0)

    for chunk in range(2):

        def part_arrive(step, carry, chunk=chunk):
            part_copy(chunk, step).wait_recv()
            return carry

        lax.fori_loop(1, exps, part_arrive, 0)
        span = slice(chunk * 2 * columns, (chunk + 1) * 2 * columns)
        total = part_send[exp, :, span].astype(f32)

        def add(step, total, span=span):
            return total + part_recv[lax.rem(exp + step, exps), :, span].astype(f32)

        total = lax.fori_loop(1, exps, add, total)
        proj_send[:, :, span] = total.astype(bf16).reshape(Z, tokens, 2 * columns)

    def proj_copy(step):
        return remote(
            proj_send.at[lax.rem(z + step, Z)],
            proj.at[z],
            proj_send_sem.at[step],
            proj_recv_sem.at[step],
            z_peer(step),
        )

    for step in range(1, Z):
        proj_copy(step).start()
    proj[z] = proj_send[z]
    for step in range(1, Z):
        proj_copy(step).wait_recv()
    for place in range(Z):
        span = slice(place * 4 * columns, (place + 1) * 4 * columns)
        out[:, span] = (residual[:, span].astype(f32) + proj[place].astype(f32)).astype(bf16)

    def kv_sent(step, carry):
        kv_copy(step).wait_send()
        kv_pass(step).wait_send()
        return carry

    lax.fori_loop(1, 8, kv_sent, 0)
    kv_pass(0).wait_send()
    w_pair.wait_send()
    w_across.wait_send()
    w_pass.wait_send()

    def att_sent(head, carry):
        for step in range(1, Z):
            att_copy(head, step).wait_send()
        return carry

    lax.fori_loop(0, heads, att_sent, 0)

    def part_sent(step, carry):
        for chunk in range(2):
            part_copy(chunk, step).wait_send()
        return carry

    lax.fori_loop(1, exps, part_sent, 0)
    for step in range(1, Z):
        proj_copy(step).wait_send()


def attention_layer(queries, key_heads, value_heads, out_proj, residual):
    bf16 = jnp.bfloat16
    tokens, width = residual.shape
    seq_rows, columns = queries.shape[0], out_proj.shape[1]
    exps = seq_rows // tokens
    head_width = key_heads.shape[1]
    heads = queries.shape[1] // head_width
    dma = pltpu.SemaphoreType.DMA
    vmem = pl.BlockSpec(memory_space=pltpu.VMEM)
    return pl.pallas_call(
        functools.partial(attention_kernel, exps),
        out_shape=jax.ShapeDtypeStruct((tokens, width), bf16),
        in_specs=[vmem] * 5,
        out_specs=vmem,
        scratch_shapes=[
            pltpu.VMEM((16, seq_rows, 2 * head_width), bf16),
            pltpu.VMEM((4,) + out_proj.shape, bf16),
            pltpu.VMEM((Z, seq_rows, heads * head_width), bf16),
            pltpu.VMEM((exps, Z * tokens, 4 * columns), bf16),
            pltpu.VMEM((exps, Z * tokens, 4 * columns), bf16),
            pltpu.VMEM((Z, tokens, 4 * columns), bf16),
            pltpu.VMEM((Z, tokens, 4 * columns), bf16),
            dma((8,)),
            dma((8,)),
            dma((8,)),
            dma((8,)),
            dma((3,)),
            dma((3,)),
            dma((3 * heads,)),
            dma((3 * heads,)),
            dma((2 * exps,)),
            dma((2 * exps,)),
            dma((Z,)),
            dma((Z,)),
            dma,
        ],
        compiler_params=pltpu.CompilerParams(
            collective_id=2, has_side_effects=True, vmem_limit_bytes=48 * 2**20
        ),
    )(queries, key_heads, value_heads, out_proj, residual)


def on_device(
    residual,
    queries,
    key_heads,
    value_heads,
    out_proj,
    norm_gain,
    gate_weight,
    up_weight,
    down_weight,
    adapter_in,
    adapter_out,
    route_ids,
    route_gates,
    adapter_mix,
):
    group_count = lax.axis_size("exp")
    tok_rows = residual.shape[0]
    hidden_state = attention_layer(queries, key_heads, value_heads, out_proj, residual)
    wide = hidden_state.astype(jnp.float32)
    normed = (
        wide * lax.rsqrt(jnp.mean(wide * wide, axis=1, keepdims=True) + 1e-05) * norm_gain
    ).astype(jnp.bfloat16)
    capacity = max(tok_rows * 5 // 16, 2 * tok_rows // group_count)
    pair_expert = route_ids.reshape(-1)
    expert_ids = jnp.arange(group_count, dtype=jnp.int32)
    onehot = (pair_expert[:, None] == expert_ids[None, :]).astype(jnp.int32)
    ranks = jnp.sum((jnp.cumsum(onehot, axis=0) - 1) * onehot, axis=1)
    target = pair_expert * capacity + ranks
    slot_ids = jnp.arange(group_count * capacity, dtype=jnp.int32)
    pair_hit = target[None, :] == slot_ids[:, None]
    pair_token = jnp.arange(2 * tok_rows, dtype=jnp.int32) // 2
    token_ids = jnp.arange(tok_rows, dtype=jnp.int32)
    pair_of_token = (pair_token[:, None] == token_ids[None, :]).astype(jnp.float32)
    placing = jnp.dot(pair_hit.astype(jnp.float32), pair_of_token).astype(jnp.bfloat16)
    send_rows = (
        jnp.dot(placing, normed, preferred_element_type=jnp.float32)
        .astype(jnp.bfloat16)
        .reshape(group_count, capacity, 2, -1, 128)
        .transpose(2, 0, 1, 3, 4)
    )
    send_mix = jnp.dot(
        placing, adapter_mix.astype(jnp.bfloat16), preferred_element_type=jnp.float32
    ).astype(jnp.bfloat16)
    tail = jnp.pad(
        send_mix.reshape(group_count, capacity, 1, -1),
        ((0, 0), (0, 0), (0, 7), (0, 128 - send_mix.shape[1])),
    )
    disp = jnp.concatenate([send_rows, jnp.broadcast_to(tail, (2,) + tail.shape)], axis=3)
    gate_flat = route_gates.reshape(-1)
    weighted = jnp.where(pair_hit, gate_flat[None, :], 0.0)
    slot_gates = jnp.dot(weighted, pair_of_token, precision=lax.Precision.HIGHEST)
    return expert_layer(
        disp,
        hidden_state,
        slot_gates.T,
        gate_weight[0],
        up_weight[0],
        down_weight[0],
        adapter_in[0],
        adapter_out[0],
    )


def solution(mesh):
    in_specs = (
        P(("seq", "exp"), None),
        P("seq", "exp"),
        P("seq", "exp"),
        P("seq", "exp"),
        P("exp", "seq"),
        P(),
        P("exp", "seq", None),
        P("exp", "seq", None),
        P("exp", "seq", None),
        P("exp", "seq", None),
        P("exp", "seq", None),
        P(("seq", "exp"), None),
        P(("seq", "exp"), None),
        P(("seq", "exp"), None),
    )
    out_specs = P(("seq", "exp"), None)
    return jax.shard_map(
        on_device, mesh=mesh, in_specs=in_specs, out_specs=out_specs, check_vma=False
    )
```

profile of v0, /device:TPU:1, one launch (start us, length us, event | category | flops | bytes accessed | tf_op | source)
XLA Modules:
  0.0 179.1 jit_solution(14273519116085584131)
XLA Ops:
  0.0 0.8 copy.18
  0.8 0.1 reshape.41
  0.8 0.1 fusion.10
  0.9 0.1 reduce_window_sum.11
  1.0 0.2 select_reduce_fusion
  1.2 0.2 convolution_convert_fusion.2
  1.4 0.0 copy-start.1
  1.4 1.1 copy-done.1
  2.5 0.0 copy-start.2
  2.5 0.9 copy-done.2
  3.4 0.0 copy-start.3
  3.4 0.9 copy-done.3
  4.4 0.0 copy-start.4
  4.4 0.8 copy-done.4
  5.1 0.0 copy-start.5
  5.1 0.8 copy-done.5
  5.9 55.6 %shard_map.136.hidden = bf16[16,6144]{1,0:T(8,128)(2,1)S(1)} custom-call(bf16[128,768]{1,0:T(8,128)(2,1)S(1)} %copy-done.2, bf16[128,128]{1,0:T(8,128)(2,1)S(1)} %copy-done.4, bf16[128,128]{1,0:T(8,128)(2,1)S(1)} %copy-done.5, bf16[768,384]{1,0:T(8,128)(2,1)S(1)} %copy-done.1, bf16[16,6144]{1,0:T(8,128)(2,1)S(1)} %copy-done.3), custom_call_target="tpu_custom_call" | custom-call | tf_op jit(solution)/shard_map/pallas_call | solution.py:786
  61.4 0.0 copy-start
  61.4 0.2 fusion.1
  61.6 1.1 fusion
  62.7 0.1 copy.23
  62.8 0.1 copy.25
  62.8 0.9 convolution_convert_fusion.1
  63.8 0.9 pad_maximum_fusion.disp
  64.7 0.8 copy.21
  65.5 0.1 broadcast_in_dim.25
  65.5 0.9 fusion.7.slot_gates
  66.4 0.0 copy-done
  66.4 111.0 %shard_map.137 = bf16[16,6144]{1,0:T(8,128)(2,1)} custom-call(bf16[2,8,5,32,128]{4,3,2,1,0:T(8,128)(2,1)} %pad_maximum_fusion.disp, bf16[16,6144]{1,0:T(8,128)(2,1)} %copy-done, f32[16,40]{1,0:T(8,128)} %fusion.7.slot_gates, bf16[512,6144]{1,0:T(8,128)(2,1)} %bitcast.14, bf16[512,6144]{1,0:T(8,128)(2,1)} %bitcast.15, bf16[512,6144]{1,0:T(8,128)(2,1)} %bitcast.16, ...), custom_call_target="tpu_custom_call" | custom-call | tf_op jit(solution)/shard_map/pallas_call | solution.py:476
  177.5 1.6 copy.27
  (5 shorter events, 0.1 us)
Async XLA Ops:
  1.4 1.1 copy-start.1
  2.5 0.9 copy-start.2
  3.4 0.9 copy-start.3
  4.4 0.8 copy-start.4
  5.1 0.8 copy-start.5
  61.4 5.0 %copy-start = (bf16[16,6144]{1,0:T(8,128)(2,1)}, bf16[16,6144]{1,0:T(8,128)(2,1)S(1)}, u32[]{:S(2)}) copy-start(bf16[16,6144]{1,0:T(8,128)(2,1)S(1)} %shard_map.136.hidden) | copy-start | bytes 589828
where the time goes:
time: 181 us; the launch traced here: 179 us
  Pallas kernels  167 us (92%)
  local copies, waits for them, and re-layouts  7.93 us (4%)
  matrix products  3.07 us (2%)
    pallas_call x1, Pallas kernels, expert_layer(): pl.pallas_call(functools.partial(expert_kernel, exps), out_shape=jax.Shap...  111 us
    pallas_call x1, Pallas kernels, attention_layer(): pl.pallas_call(functools.partial(attention_kernel, exps), out_shape=jax.S...  55.6 us
    unnamed x16, local copies, waits for them, and re-layouts  7.65 us

commit v1 on v0

v1 whole, which is shorter than its diff:
```python
import functools

import jax
import jax.numpy as jnp
from jax import lax
from jax.experimental import pallas as pl
from jax.experimental.pallas import tpu as pltpu
from jax.sharding import PartitionSpec as P

RANK = 16


MESH = pl.DeviceIdType.MESH
CAP = 5
Z = 4
PIECES = 3
SLOT_ROWS = 16


def dot(left, right):
    return jnp.dot(left, right, preferred_element_type=jnp.float32)


def contract_last(left, right):
    return lax.dot_general(
        left, right, (((1,), (1,)), ((), ())), preferred_element_type=jnp.float32
    )


def tile_of(size, most):
    while size % most:
        most -= 128
    return most


def place_on_mesh():
    me = lax.axis_index("seq")
    core = lax.rem(me, 2)
    x_hi = lax.rem(me // 2, 2)
    z = me // 4
    return me, z, x_hi, core


def seq_of(z, x_hi, core):
    return lax.rem(z + Z, Z) * 4 + x_hi * 2 + core


def expert_kernel(
    exps,
    hidden,
    gain,
    ids,
    route_gates,
    mix,
    gate_hbm,
    up_hbm,
    down_hbm,
    in_hbm,
    out_hbm,
    out,
    placed_wide,
    disp,
    arrived,
    wide_slots,
    rows,
    w_first,
    w_second,
    units,
    pair_send,
    pair_recv,
    own,
    z_send,
    half_low,
    half_high,
    full_low,
    full_high,
    x_send,
    x_recv,
    wide_send,
    wide_recv,
    back_wide,
    back,
    returned,
    returned_wide,
    returned_rows,
    weight_sems,
    send_sems,
    recv_sems,
    disp_send,
    disp_recv,
    back_send,
    back_recv,
    local_sems,
):
    bf16, f32 = jnp.bfloat16, jnp.float32
    tokens, width = hidden.shape
    half = width // 2
    lanes = half // 128
    run = lanes // PIECES
    piece = run * 128
    hidden_units = gate_hbm.shape[0]
    adapters = in_hbm.shape[0]
    block = 2 * exps * CAP
    many = 4 * block
    peers = 2 * exps
    slots = exps * CAP
    mix_width = mix.shape[1]

    me, z, x_hi, core = place_on_mesh()
    exp = lax.axis_index("exp")
    sibling = (seq_of(z, x_hi, 1 - core), exp)
    above = (seq_of(z + 1, x_hi, core), exp)
    below = (seq_of(z - 1, x_hi, core), exp)
    across = (seq_of(z, 1 - x_hi, core), exp)
    mine = core * exps + exp

    def peer(step):
        at = lax.rem(mine + step, peers)
        return at, (seq_of(z, x_hi, at // exps), lax.rem(at, exps))

    barrier = pltpu.get_barrier_semaphore()

    def greet(step, carry):
        pl.semaphore_signal(barrier, inc=1, device_id=peer(step)[1], device_id_type=MESH)
        return carry

    lax.fori_loop(1, peers, greet, 0)
    for other in (above, below, across):
        pl.semaphore_signal(barrier, inc=1, device_id=other, device_id_type=MESH)

    loads = []
    for side in range(2):
        columns = pl.ds(side * half, half)
        for source, place, start in (
            (gate_hbm, w_first, 0),
            (up_hbm, w_first, hidden_units),
            (in_hbm, w_first, 2 * hidden_units),
            (down_hbm, w_second, 0),
            (out_hbm, w_second, hidden_units),
        ):
            load = pltpu.make_async_copy(
                source.at[:, columns],
                place.at[side, pl.ds(start, source.shape[0]), :],
                weight_sems.at[len(loads)],
            )
            load.start()
            loads.append(load)

    first_row, second_row = ids[0:1, :], ids[1:2, :]
    down_at = lax.broadcasted_iota(jnp.int32, (tokens, tokens), 0)
    along_at = lax.broadcasted_iota(jnp.int32, (tokens, tokens), 1)

    def upright(row):
        return jnp.sum(jnp.where(down_at == along_at, row, 0), axis=1, keepdims=True)

    first, second = upright(first_row), upright(second_row)

    def count(hits, axis):
        return jnp.sum(jnp.where(hits, 1, 0), axis=axis, keepdims=True)

    first_slot_row = first_row * CAP + count((first == first_row) & (down_at < along_at), 0)
    second_slot_row = (
        second_row * CAP
        + count(first == second_row, 0)
        + count((second == second_row) & (down_at < along_at), 0)
    )
    first_slot = first * CAP + count((first == first_row) & (along_at < down_at), 1)
    second_slot = (
        second * CAP
        + count(second == first_row, 1)
        + count((second == second_row) & (along_at < down_at), 1)
    )
    slot_at = lax.broadcasted_iota(jnp.int32, (slots, tokens), 0)
    placing = jnp.where(
        (slot_at == first_slot_row) | (slot_at == second_slot_row), 1.0, 0.0
    ).astype(bf16)
    slot_along = lax.broadcasted_iota(jnp.int32, (tokens, slots), 1)
    slot_gates = jnp.where(slot_along == first_slot, upright(route_gates[0:1, :]), 0.0) + jnp.where(
        slot_along == second_slot, upright(route_gates[1:2, :]), 0.0
    )
    gate_high = slot_gates.astype(bf16)
    rest = slot_gates - gate_high.astype(f32)
    gate_mid = rest.astype(bf16)
    gate_low = (rest - gate_mid.astype(f32)).astype(bf16)

    wide = hidden[...].astype(f32)
    scale = lax.rsqrt(jnp.mean(wide * wide, axis=1, keepdims=True) + 1e-05)

    def place_columns(side, lane):
        columns = slice(side * half + lane * 128, side * half + (lane + 1) * 128)
        normed = (hidden[:, columns].astype(f32) * scale * gain[:, columns]).astype(bf16)
        return dot(placing, normed)

    placed_wide[...] = jnp.zeros_like(placed_wide)
    mix_rows = dot(placing, mix[...].astype(f32).astype(bf16))
    for side in range(2):
        for lane in range(lanes):
            part, at = (0, lane) if lane < run else (1, lane - run)
            start = (side * 2 + part) * slots * SLOT_ROWS + at
            placed_wide[pl.ds(start, slots, stride=SLOT_ROWS), :] = place_columns(side, lane)
        start = side * 2 * slots * SLOT_ROWS + run
        placed_wide[pl.ds(start, slots, stride=SLOT_ROWS), 0:mix_width] = mix_rows
    disp[...] = placed_wide[...].reshape(disp.shape).astype(bf16)

    pl.semaphore_wait(barrier, peers - 1 + 3)

    def remote(source, target, send, recv, device):
        return pltpu.make_async_remote_copy(
            src_ref=source,
            dst_ref=target,
            send_sem=send,
            recv_sem=recv,
            device_id=device,
            device_id_type=MESH,
        )

    started = []

    def begin(source, target, device):
        index = len(started)
        copy = remote(source, target, send_sems.at[index], recv_sems.at[index], device)
        copy.start()
        started.append(copy)
        return copy

    def dispatch(part, step):
        at, device = peer(step)
        return remote(
            disp.at[at // exps, part, lax.rem(at, exps)],
            arrived.at[part, mine],
            disp_send.at[part, step],
            disp_recv.at[part, step],
            device,
        )

    keeps = []
    for part in range(2):

        def dispatch_start(step, carry, part=part):
            dispatch(part, step).start()
            return carry

        lax.fori_loop(1, peers, dispatch_start, 0)
        keep = pltpu.make_async_copy(
            disp.at[core, part, exp], arrived.at[part, mine], local_sems.at[part]
        )
        keep.start()
        keeps.append(keep)

    edges = [0] + [128 + (index + 1) * piece for index in range(PIECES)]
    middles = [
        edges[index] + (edges[index + 1] - edges[index]) // 256 * 128 for index in range(PIECES)
    ]

    def land(part):
        def dispatch_wait(step, carry):
            dispatch(part, step).wait_recv()
            return carry

        lax.fori_loop(1, peers, dispatch_wait, 0)
        keeps[part].wait()
        wide_slots[part] = arrived[part].astype(f32).reshape(block * SLOT_ROWS, 128)
        chosen = [(run, 0)] + [(lane, lane + 1) for lane in range(run)]
        if part == 1:
            chosen = [(lane, run + 1 + lane) for lane in range(lanes - run)]
        for source, target in chosen:
            rows[core, 0:block, target * 128 : (target + 1) * 128] = wide_slots[
                part, pl.ds(source, block, stride=SLOT_ROWS), :
            ].astype(bf16)

    def cell(place, start, stop):
        return rows.at[core, pl.ds(place * block, block), pl.ds(start, stop - start)]

    def move(source, target, index, device, which=None):
        start, stop = edges[index], edges[index + 1]
        if which == 0:
            stop = middles[index]
        if which == 1:
            start = middles[index]
        return begin(cell(source, start, stop), cell(target, start, stop), device)

    handed = {}

    def hand_over(place, index):
        handed[place, index] = move(place, place, index, sibling)

    low, high, opposite, crossed = {}, {}, {}, {}

    def ring_own(index):
        low[0, index] = move(0, 1, index, above)
        high[0, index] = move(0, 2, index, below)

    def cross_own(index):
        crossed[0, index] = move(0, 4, index, across)
        hand_over(0, index)

    def relay(base, index):
        low[base, index].wait_recv()
        opposite[base, index, 0] = move(base + 1, base + 3, index, above, 0)
        if index == 0:
            crossed[1, 0] = move(1, 5, 0, across)
        hand_over(base + 1, index)
        high[base, index].wait_recv()
        opposite[base, index, 1] = move(base + 2, base + 3, index, below, 1)
        if index == 0:
            crossed[2, 0] = move(2, 6, 0, across)
        hand_over(base + 2, index)

    def close(base, index):
        opposite[base, index, 0].wait_recv()
        opposite[base, index, 1].wait_recv()
        if index == 0:
            crossed[3, 0] = move(3, 7, 0, across)
        hand_over(base + 3, index)

    def spread_crossed(index):
        crossed[0, index].wait_recv()
        low[4, index] = move(4, 5, index, above)
        high[4, index] = move(4, 6, index, below)
        hand_over(4, index)

    def take_crossed(place):
        crossed[place, 0].wait_recv()
        hand_over(place + 4, 0)

    land(0)
    ring_own(0)
    land(1)
    for index in range(1, PIECES):
        cross_own(index)
    cross_own(0)
    relay(0, 0)
    spread_crossed(1)
    spread_crossed(2)
    close(0, 0)
    ring_own(1)
    relay(4, 1)
    ring_own(2)
    relay(4, 2)
    for place in range(4):
        take_crossed(place)
    for index in range(1, PIECES):
        close(4, index)

    for load in loads:
        load.wait()
    unit_tile = tile_of(hidden_units, 256)
    adapter_at = lax.broadcasted_iota(jnp.int32, (mix_width, adapters), 1) // RANK
    spread = (
        lax.broadcasted_iota(jnp.int32, (mix_width, adapters), 0)
        == adapter_at + me * (adapters // RANK)
    ).astype(bf16)

    def first_layer(group, between):
        at = pl.ds(group * many, many)
        data = pl.ds(128, half)

        def project(start, size):
            return contract_last(
                rows[0, at, data], w_first[0, pl.ds(start, size), :]
            ) + contract_last(rows[1, at, data], w_first[1, pl.ds(start, size), :])

        scales = dot(rows[0, at, 0:mix_width], spread) / 8.0
        units[:, hidden_units : hidden_units + adapters] = (
            project(2 * hidden_units, adapters) * scales
        ).astype(bf16)
        for start in range(0, hidden_units, unit_tile):
            gate = project(start, unit_tile)
            between[0]()
            upward = project(hidden_units + start, unit_tile)
            units[:, start : start + unit_tile] = (jax.nn.silu(gate) * upward).astype(bf16)
            between[1]()
            between = between[2:]

    out_tile = tile_of(piece, 512)

    def second_layer(group, side, index, target):
        def tile(step, carry):
            start = pl.multiple_of(index * piece + step * out_tile, 128)
            value = dot(units[...], w_second[side, :, pl.ds(start, out_tile)])
            target[group, :, pl.ds(start, out_tile)] = value.astype(target.dtype)
            return carry

        lax.fori_loop(0, piece // out_tile, tile, 0)

    def columns_of(index, which=None):
        start, stop = index * piece, (index + 1) * piece
        middle = start + piece // 256 * 128
        if which == 0:
            stop = middle
        if which == 1:
            start = middle
        return pl.ds(start, stop - start)

    swaps = {}

    def to_sibling(group, index):
        second_layer(group, 1 - core, index, pair_send)
        at = columns_of(index)
        swaps[group, index] = begin(
            pair_send.at[group, :, at], pair_recv.at[group, :, at], sibling
        )

    def pair_sum(group, place, index, which=None):
        columns = columns_of(index, which)
        inner = columns_of(0, which)
        at = pl.ds(place * block, block)
        total = own[group, at, columns] + pair_recv[group, at, columns].astype(f32)
        if group == 0 and index == 0:
            total = total + wide_recv[at, inner].astype(f32)
        return total

    flows = {}

    def z_flow(group, index, place, which, target, device):
        at = columns_of(index, which)
        return begin(z_send.at[group, place - 1, :, at], target.at[group, :, at], device)

    def reduce_own(group, index):
        second_layer(group, core, index, own)
        swaps[group, index].wait_recv()
        both, left, right = (columns_of(index, which) for which in (None, 0, 1))
        z_send[group, 2, :, both] = pair_sum(group, 3, index).astype(bf16)
        flows["half_low", group, index] = z_flow(group, index, 3, 0, half_low, above)
        flows["half_high", group, index] = z_flow(group, index, 3, 1, half_high, below)
        z_send[group, 1, :, right] = pair_sum(group, 2, index, 1).astype(bf16)
        flows["low_1", group, index] = z_flow(group, index, 2, 1, full_low, above)
        z_send[group, 0, :, left] = pair_sum(group, 1, index, 0).astype(bf16)
        flows["high_0", group, index] = z_flow(group, index, 1, 0, full_high, below)
        own[group, 2 * block : 3 * block, left] = pair_sum(group, 2, index, 0)
        own[group, block : 2 * block, right] = pair_sum(group, 1, index, 1)
        own[group, 0:block, both] = pair_sum(group, 0, index)

    def pass_on(group, index):
        left, right = columns_of(index, 0), columns_of(index, 1)
        flows["half_low", group, index].wait_recv()
        z_send[group, 1, :, left] = (
            own[group, 2 * block : 3 * block, left] + half_low[group, :, left].astype(f32)
        ).astype(bf16)
        flows["low_0", group, index] = z_flow(group, index, 2, 0, full_low, above)
        flows["half_high", group, index].wait_recv()
        z_send[group, 0, :, right] = (
            own[group, block : 2 * block, right] + half_high[group, :, right].astype(f32)
        ).astype(bf16)
        flows["high_1", group, index] = z_flow(group, index, 1, 1, full_high, below)

    def settled(group, index):
        for name in ("low_0", "low_1", "high_0", "high_1"):
            flows[name, group, index].wait_recv()
        both = columns_of(index)
        return (
            own[group, 0:block, both]
            + full_low[group, :, both].astype(f32)
            + full_high[group, :, both].astype(f32)
        )

    def all_here(group):
        for place in range(4):
            for index in range(PIECES):
                handed[group * 4 + place, index].wait_recv()

    def nothing():
        return None

    def cross_wide():
        second_layer(1, core, 0, own)
        swaps[1, 0].wait_recv()
        for place in range(4):
            wide_send[place * block : (place + 1) * block, :] = pair_sum(
                1, place, 0
            ).astype(bf16)
        flows["wide"] = begin(wide_send, wide_recv, across)

    crossing = {}

    def cross_settled(index):
        at = columns_of(index)
        x_send[:, at] = settled(1, index).astype(bf16)
        crossing[index] = begin(x_send.at[:, at], x_recv.at[:, at], across)

    all_here(1)
    first_layer(
        1,
        [lambda: relay(0, 1), nothing, lambda: relay(0, 2), nothing],
    )
    to_sibling(1, 0)
    to_sibling(1, 1)
    cross_wide()
    to_sibling(1, 2)
    close(0, 1)
    reduce_own(1, 1)
    close(0, 2)
    reduce_own(1, 2)
    all_here(0)
    first_layer(
        0,
        [lambda: pass_on(1, 1), nothing, lambda: pass_on(1, 2), nothing],
    )
    to_sibling(0, 1)
    to_sibling(0, 2)
    reduce_own(0, 1)
    to_sibling(0, 0)
    reduce_own(0, 2)
    cross_settled(1)
    flows["wide"].wait_recv()
    reduce_own(0, 0)
    cross_settled(2)
    for index in (1, 2, 0):
        pass_on(0, index)

    def give_back(index, step):
        at, device = peer(step)
        return remote(
            back.at[index, at],
            returned.at[index, core, exp],
            back_send.at[index, step],
            back_recv.at[index, step],
            device,
        )

    keeps_back = {}
    for index in (1, 2, 0):
        own[0, 0:block, columns_of(index)] = settled(0, index)
        if index > 0:
            crossing[index].wait_recv()
        for lane in range(run):
            columns = slice(index * piece + lane * 128, index * piece + (lane + 1) * 128)
            value = own[0, 0:block, columns]
            if index > 0:
                value = value + x_recv[:, columns].astype(f32)
            back_wide[index, pl.ds(lane, block, stride=run), :] = value
        back[index] = back_wide[index].reshape(back.shape[1:]).astype(bf16)

        def give_start(step, carry, index=index):
            give_back(index, step).start()
            return carry

        lax.fori_loop(1, peers, give_start, 0)
        keep = pltpu.make_async_copy(
            back.at[index, mine], returned.at[index, core, exp], local_sems.at[2 + index]
        )
        keep.start()
        keeps_back[index] = keep

    for copy in started:
        copy.wait_send()
    for part in range(2):

        def dispatch_sent(step, carry, part=part):
            dispatch(part, step).wait_send()
            return carry

        lax.fori_loop(1, peers, dispatch_sent, 0)
    stacked = jnp.concatenate(
        [gate_high.astype(f32), gate_mid.astype(f32), gate_low.astype(f32)], axis=0
    ).astype(bf16)
    for index in (1, 2, 0):

        def give_wait(step, carry, index=index):
            give_back(index, step).wait()
            return carry

        lax.fori_loop(1, peers, give_wait, 0)
        keeps_back[index].wait()
        returned_wide[...] = returned[index].astype(f32).reshape(2 * slots * run, 128)
        for side in range(2):
            for lane in range(run):
                returned_rows[side, :, lane * 128 : (lane + 1) * 128] = returned_wide[
                    pl.ds(side * slots * run + lane, slots, stride=run), :
                ].astype(bf16)
            routed = dot(stacked, returned_rows[side])
            routed = routed[0:tokens] + (
                routed[tokens : 2 * tokens] + routed[2 * tokens : 3 * tokens]
            )
            columns = slice(side * half + index * piece, side * half + (index + 1) * piece)
            out[:, columns] = (hidden[:, columns].astype(f32) + routed).astype(bf16)


def expert_layer(
    hidden, gain, ids, route_gates, mix, gate, up, down, adapter_in, adapter_out, exps
):
    bf16, f32 = jnp.bfloat16, jnp.float32
    tokens, width = hidden.shape
    half = width // 2
    lanes = half // 128
    run = lanes // PIECES
    block = 2 * exps * CAP
    slots = exps * CAP
    hidden_units, adapters = gate.shape[0], adapter_in.shape[0]
    inner = hidden_units + adapters
    dma = pltpu.SemaphoreType.DMA
    vmem = pl.BlockSpec(memory_space=pltpu.VMEM)
    anywhere = pl.BlockSpec(memory_space=pl.ANY)
    return pl.pallas_call(
        functools.partial(expert_kernel, exps),
        out_shape=jax.ShapeDtypeStruct((tokens, width), bf16),
        in_specs=[vmem] * 5 + [anywhere] * 5,
        out_specs=vmem,
        scratch_shapes=[
            pltpu.VMEM((2 * 2 * slots * SLOT_ROWS, 128), f32),
            pltpu.VMEM((2, 2, exps, CAP, SLOT_ROWS, 128), bf16),
            pltpu.VMEM((2, 2 * exps, CAP, SLOT_ROWS, 128), bf16),
            pltpu.VMEM((2, block * SLOT_ROWS, 128), f32),
            pltpu.VMEM((2, 8 * block, half + 128), bf16),
            pltpu.VMEM((2, hidden_units + inner, half), bf16),
            pltpu.VMEM((2, inner, half), bf16),
            pltpu.VMEM((4 * block, inner), bf16),
            pltpu.VMEM((2, 4 * block, half), bf16),
            pltpu.VMEM((2, 4 * block, half), bf16),
            pltpu.VMEM((2, 4 * block, half), f32),
            pltpu.VMEM((2, 3, block, half), bf16),
            pltpu.VMEM((2, block, half), bf16),
            pltpu.VMEM((2, block, half), bf16),
            pltpu.VMEM((2, block, half), bf16),
            pltpu.VMEM((2, block, half), bf16),
            pltpu.VMEM((block, half), bf16),
            pltpu.VMEM((block, half), bf16),
            pltpu.VMEM((4 * block, run * 128), bf16),
            pltpu.VMEM((4 * block, run * 128), bf16),
            pltpu.VMEM((PIECES, block * run, 128), f32),
            pltpu.VMEM((PIECES, 2 * exps, CAP, run, 128), bf16),
            pltpu.VMEM((PIECES, 2, exps, CAP, run, 128), bf16),
            pltpu.VMEM((2 * slots * run, 128), f32),
            pltpu.VMEM((2, slots, run * 128), bf16),
            dma((10,)),
            dma((108,)),
            dma((108,)),
            dma((2, 2 * exps)),
            dma((2, 2 * exps)),
            dma((PIECES, 2 * exps)),
            dma((PIECES, 2 * exps)),
            dma((2 + PIECES,)),
        ],
        compiler_params=pltpu.CompilerParams(
            collective_id=1, has_side_effects=True, vmem_limit_bytes=62 * 2**20
        ),
    )(
        hidden,
        gain.reshape(1, width),
        ids.T,
        route_gates.T,
        mix,
        gate,
        up,
        down,
        adapter_in,
        adapter_out,
    )


def attention_kernel(
    exps,
    queries,
    key_heads,
    value_heads,
    out_proj,
    residual,
    out,
    held_queries,
    held_residual,
    pairs,
    weights,
    attended,
    part_send,
    part_recv,
    proj_send,
    proj,
    send_sems,
    recv_sems,
    att_send,
    att_recv,
    part_send_sem,
    part_recv_sem,
    proj_send_sem,
    proj_recv_sem,
    local_sems,
):
    bf16, f32 = jnp.bfloat16, jnp.float32
    seq_rows = queries.shape[0]
    head_width = key_heads.shape[1]
    heads = queries.shape[1] // head_width
    tokens = seq_rows // exps
    columns = out_proj.shape[1]
    length = 16 * seq_rows

    me, z, x_hi, core = place_on_mesh()
    exp = lax.axis_index("exp")
    sibling = (seq_of(z, x_hi, 1 - core), exp)
    across = (seq_of(z, 1 - x_hi, core), exp)
    mine = x_hi * 2 + core
    other = (1 - x_hi) * 2 + core

    def z_peer(step):
        return seq_of(z + step, x_hi, core), exp

    def exp_peer(step):
        return me, lax.rem(exp + step, exps)

    barrier = pltpu.get_barrier_semaphore()

    def greet_exp(step, carry):
        pl.semaphore_signal(barrier, inc=1, device_id=exp_peer(step), device_id_type=MESH)
        return carry

    for device in (across, sibling) + tuple(z_peer(step) for step in range(1, Z)):
        pl.semaphore_signal(barrier, inc=1, device_id=device, device_id_type=MESH)
    lax.fori_loop(1, exps, greet_exp, 0)
    loads = []
    for source, target in (
        (key_heads, pairs.at[me, :, pl.ds(0, head_width)]),
        (value_heads, pairs.at[me, :, pl.ds(head_width, head_width)]),
        (queries, held_queries),
        (out_proj, weights.at[mine]),
        (residual, held_residual),
    ):
        load = pltpu.make_async_copy(source, target, local_sems.at[len(loads)])
        load.start()
        loads.append(load)
    pl.semaphore_wait(barrier, 2 + Z - 1 + exps - 1)

    def remote(source, target, send, recv, device):
        return pltpu.make_async_remote_copy(
            src_ref=source,
            dst_ref=target,
            send_sem=send,
            recv_sem=recv,
            device_id=device,
            device_id_type=MESH,
        )

    started = []

    def begin(source, target, device):
        index = len(started)
        copy = remote(source, target, send_sems.at[index], recv_sems.at[index], device)
        copy.start()
        started.append(copy)
        return copy

    def send_pairs(place, device):
        return begin(pairs.at[place], pairs.at[place], device)

    loads[0].wait()
    loads[1].wait()
    beside = seq_of(z, 1 - x_hi, core)
    crossing = send_pairs(me, across)
    rings = [(step, x_hi, send_pairs(me, z_peer(step))) for step in (1, 3, 2)]
    handed = [send_pairs(me, sibling)]
    crossing.wait_recv()
    rings += [(step, 1 - x_hi, send_pairs(beside, z_peer(step))) for step in (1, 3, 2)]
    handed.append(send_pairs(beside, sibling))

    half_depth = out_proj.shape[0] // 2
    tops = [pl.ds(0, half_depth), pl.ds(half_depth, half_depth)]
    w_across = [begin(out_proj.at[top, :], weights.at[mine, top, :], across) for top in tops]
    w_pair = begin(out_proj, weights.at[mine], sibling)

    for step, side, copy in rings:
        copy.wait_recv()
        handed.append(send_pairs(seq_of(z - step + Z, side, core), sibling))
    for copy in handed:
        copy.wait_recv()
    loads[2].wait()

    scaling = head_width ** (-0.5)
    allowed = lax.broadcasted_iota(jnp.int32, (seq_rows, length), 1) <= (
        lax.broadcasted_iota(jnp.int32, (seq_rows, length), 0) + me * seq_rows
    )

    def att_copy(head, step):
        at = attended.at[z, :, pl.ds(pl.multiple_of(head * head_width, 128), head_width)]
        index = (step - 1) * heads + head
        return remote(at, at, att_send.at[index], att_recv.at[index], z_peer(step))

    def one_head(head, carry):
        span = pl.ds(pl.multiple_of(head * head_width, 128), head_width)
        all_keys = pairs[:, :, 0:head_width].reshape(length, head_width)
        scores = contract_last(held_queries[:, span], all_keys) * scaling
        scores = jnp.where(allowed, scores, -1e30)
        highest = jnp.max(scores, axis=1, keepdims=True)
        probs = jnp.exp(scores - highest)
        totals = jnp.sum(probs, axis=1, keepdims=True)
        all_values = pairs[:, :, head_width : 2 * head_width].reshape(length, head_width)
        summed = dot(probs.astype(bf16), all_values)
        attended[z, :, span] = (summed / totals).astype(bf16)
        for step in range(1, Z):
            att_copy(head, step).start()
        return carry

    lax.fori_loop(0, heads, one_head, 0)

    def att_arrive(head, carry):
        for step in range(1, Z):
            att_copy(head, step).wait_recv()
        return carry

    lax.fori_loop(0, heads, att_arrive, 0)

    def part_copy(chunk, first, step):
        to = lax.rem(exp + step, exps)
        span = halves(chunk)
        index = first * exps + step
        return remote(
            part_send.at[to, :, span],
            part_recv.at[exp, :, span],
            part_send_sem.at[index],
            part_recv_sem.at[index],
            exp_peer(step),
        )

    def halves(chunk):
        return pl.ds(pl.multiple_of(chunk * 2 * columns, 128), 2 * columns)

    def project(chunk, first):
        for piece in range(2):
            block = chunk * 2 + piece
            at = pl.ds(pl.multiple_of(block * columns, 128), columns)
            rows = attended[...].reshape(Z * seq_rows, heads * head_width)
            value = dot(rows, weights[block]).astype(bf16)
            for z_to in range(Z):
                for exp_to in range(exps):
                    start = z_to * seq_rows + exp_to * tokens
                    part_send[exp_to, z_to * tokens : (z_to + 1) * tokens, at] = value[
                        start : start + tokens
                    ]

        def part_start(step, carry):
            part_copy(chunk, first, step).start()
            return carry

        lax.fori_loop(1, exps, part_start, 0)

    def total_of(chunk, first):
        def part_arrive(step, carry):
            part_copy(chunk, first, step).wait_recv()
            return carry

        lax.fori_loop(1, exps, part_arrive, 0)
        span = halves(chunk)

        def add(step, total):
            return total + part_recv[lax.rem(exp + step, exps), :, span].astype(f32)

        total = lax.fori_loop(1, exps, add, part_send[exp, :, span].astype(f32))
        proj_send[:, :, span] = total.astype(bf16).reshape(Z, tokens, 2 * columns)

    loads[3].wait()
    w_pair.wait_recv()
    project(x_hi, 0)
    w_pass = []
    for index, top in enumerate(tops):
        w_across[index].wait_recv()
        at = weights.at[other, top, :]
        w_pass.append(begin(at, at, sibling))
    for copy in w_pass:
        copy.wait_recv()
    project(1 - x_hi, 1)
    total_of(x_hi, 0)
    total_of(1 - x_hi, 1)
    loads[4].wait()

    def proj_copy(step):
        return remote(
            proj_send.at[lax.rem(z + step, Z)],
            proj.at[z],
            proj_send_sem.at[step],
            proj_recv_sem.at[step],
            z_peer(step),
        )

    for step in range(1, Z):
        proj_copy(step).start()
    proj[z] = proj_send[z]
    for step in range(1, Z):
        proj_copy(step).wait_recv()
    for place in range(Z):
        span = slice(place * 4 * columns, (place + 1) * 4 * columns)
        out[:, span] = (held_residual[:, span].astype(f32) + proj[place].astype(f32)).astype(bf16)

    for copy in started:
        copy.wait_send()

    def att_sent(head, carry):
        for step in range(1, Z):
            att_copy(head, step).wait_send()
        return carry

    lax.fori_loop(0, heads, att_sent, 0)

    def part_sent(step, carry):
        part_copy(x_hi, 0, step).wait_send()
        part_copy(1 - x_hi, 1, step).wait_send()
        return carry

    lax.fori_loop(1, exps, part_sent, 0)
    for step in range(1, Z):
        proj_copy(step).wait_send()


def attention_layer(queries, key_heads, value_heads, out_proj, residual):
    bf16 = jnp.bfloat16
    tokens, width = residual.shape
    seq_rows, columns = queries.shape[0], out_proj.shape[1]
    exps = seq_rows // tokens
    head_width = key_heads.shape[1]
    heads = queries.shape[1] // head_width
    dma = pltpu.SemaphoreType.DMA
    vmem = pl.BlockSpec(memory_space=pltpu.VMEM)
    return pl.pallas_call(
        functools.partial(attention_kernel, exps),
        out_shape=jax.ShapeDtypeStruct((tokens, width), bf16),
        in_specs=[pl.BlockSpec(memory_space=pl.ANY)] * 5,
        out_specs=vmem,
        scratch_shapes=[
            pltpu.VMEM(queries.shape, bf16),
            pltpu.VMEM(residual.shape, bf16),
            pltpu.VMEM((16, seq_rows, 2 * head_width), bf16),
            pltpu.VMEM((4,) + out_proj.shape, bf16),
            pltpu.VMEM((Z, seq_rows, heads * head_width), bf16),
            pltpu.VMEM((exps, Z * tokens, 4 * columns), bf16),
            pltpu.VMEM((exps, Z * tokens, 4 * columns), bf16),
            pltpu.VMEM((Z, tokens, 4 * columns), bf16),
            pltpu.VMEM((Z, tokens, 4 * columns), bf16),
            dma((20,)),
            dma((20,)),
            dma((3 * heads,)),
            dma((3 * heads,)),
            dma((2 * exps,)),
            dma((2 * exps,)),
            dma((Z,)),
            dma((Z,)),
            dma((5,)),
        ],
        compiler_params=pltpu.CompilerParams(
            collective_id=2, has_side_effects=True, vmem_limit_bytes=62 * 2**20
        ),
    )(queries, key_heads, value_heads, out_proj, residual)


def on_device(
    residual,
    queries,
    key_heads,
    value_heads,
    out_proj,
    norm_gain,
    gate_weight,
    up_weight,
    down_weight,
    adapter_in,
    adapter_out,
    route_ids,
    route_gates,
    adapter_mix,
):
    hidden_state = attention_layer(queries, key_heads, value_heads, out_proj, residual)
    return expert_layer(
        hidden_state,
        norm_gain,
        route_ids,
        route_gates,
        adapter_mix,
        gate_weight[0],
        up_weight[0],
        down_weight[0],
        adapter_in[0],
        adapter_out[0],
        lax.axis_size("exp"),
    )


def solution(mesh):
    in_specs = (
        P(("seq", "exp"), None),
        P("seq", "exp"),
        P("seq", "exp"),
        P("seq", "exp"),
        P("exp", "seq"),
        P(),
        P("exp", "seq", None),
        P("exp", "seq", None),
        P("exp", "seq", None),
        P("exp", "seq", None),
        P("exp", "seq", None),
        P(("seq", "exp"), None),
        P(("seq", "exp"), None),
        P(("seq", "exp"), None),
    )
    out_specs = P(("seq", "exp"), None)
    return jax.shard_map(
        on_device, mesh=mesh, in_specs=in_specs, out_specs=out_specs, check_vma=False
    )
```

time: 181 us -> 154 us (0.85)
  Pallas kernels: 167 us -> 152 us
  local copies, waits for them, and re-layouts: 7.93 us -> 1.62 us
  matrix products: 3.07 us -> 0 us
    pallas_call x1, Pallas kernels: 111 us -> 96.9 us  [expert_layer(): pl.pallas_call(functools.partial(expert_kernel, exps), out_shape=jax.Shap...]
    unnamed x16 -> x1, local copies, waits for them, and re-layouts: 7.65 us -> 1.62 us
    dot_general x4 -> x0, matrix products: 3.07 us -> none  [the longest x1 1.08 us: on_device(): jnp.dot(placing, normed, preferred_element_type=jnp.float32)]
where the time goes in v1:
time: 154 us
  Pallas kernels  152 us (99%)
  local copies, waits for them, and re-layouts  1.62 us (1%)
    pallas_call x1, Pallas kernels, expert_layer(): pl.pallas_call(functools.partial(expert_kernel, exps), out_shape=jax.Shap...  96.9 us
    pallas_call x1, Pallas kernels, attention_layer(): pl.pallas_call(functools.partial(attention_kernel, exps), out_shape=jax.S...  55.3 us

profile of v1, /device:TPU:1, one launch (start us, length us, event | category | flops | bytes accessed | tf_op | source)
XLA Modules:
  0.0 153.8 jit_solution(2042905505160143649)
XLA Ops:
  0.0 55.3 %shard_map.136.hidden = bf16[16,6144]{1,0:T(8,128)(2,1)} custom-call(bf16[128,768]{1,0:T(8,128)(2,1)} %queries.1, bf16[128,128]{1,0:T(8,128)(2,1)} %key_heads.1, bf16[128,128]{1,0:T(8,128)(2,1)} %value_heads.1, bf16[768,384]{1,0:T(8,128)(2,1)} %out_proj.1, bf16[16,6144]{1,0:T(8,128)(2,1)} %residual.1), custom_call_target="tpu_custom_call" | custom-call | tf_op jit(solution)/shard_map/pallas_call | solution.py:909
  55.3 96.9 %shard_map.137 = bf16[16,6144]{1,0:T(8,128)(2,1)} custom-call(bf16[16,6144]{1,0:T(8,128)(2,1)} %shard_map.136.hidden, f32[1,6144]{1,0:T(1,128)} %bitcast.13, s32[2,16]{1,0:T(2,128)} %bitcast.14, f32[2,16]{1,0:T(2,128)} %bitcast.15, s32[16,64]{1,0:T(8,128)} %mix.1, bf16[512,6144]{1,0:T(8,128)(2,1)} %bitcast.8, bf16[512,6144]{1,0:T(8,128)(2,1)} %bitcast.9, ...), custom_call_target="tpu_custom_call" | custom-call | tf_op jit(solution)/shard_map/pallas_call | solution.py:594
  152.2 1.6 %copy.16 = bf16[16,6144]{1,0:T(8,128)(2,1)} copy(bf16[16,6144]{1,0:T(8,128)(2,1)} %shard_map.137) | data formatting | bytes 393216

commit v2 on v1

--- a/solution.py
+++ b/solution.py
@@ -328,14 +328,14 @@
     land(1)
     for index in range(1, PIECES):
         cross_own(index)
+    ring_own(1)
     cross_own(0)
     relay(0, 0)
     spread_crossed(1)
     spread_crossed(2)
+    ring_own(2)
     close(0, 0)
-    ring_own(1)
     relay(4, 1)
-    ring_own(2)
     relay(4, 2)
     for place in range(4):
         take_crossed(place)
@@ -372,7 +372,7 @@
             between[1]()
             between = between[2:]
 
-    out_tile = tile_of(piece, 512)
+    out_tile = tile_of(piece, 1024)
 
     def second_layer(group, side, index, target):
         def tile(step, carry):
@@ -665,6 +665,10 @@
     part_recv,
     proj_send,
     proj,
+    kv_send,
+    kv_recv,
+    pass_send,
+    pass_recv,
     send_sems,
     recv_sems,
     att_send,
@@ -687,6 +691,7 @@
     exp = lax.axis_index("exp")
     sibling = (seq_of(z, x_hi, 1 - core), exp)
     across = (seq_of(z, 1 - x_hi, core), exp)
+    chip = z * 2 + x_hi
     mine = x_hi * 2 + core
     other = (1 - x_hi) * 2 + core
 
@@ -702,8 +707,16 @@
         pl.semaphore_signal(barrier, inc=1, device_id=exp_peer(step), device_id_type=MESH)
         return carry
 
-    for device in (across, sibling) + tuple(z_peer(step) for step in range(1, Z)):
-        pl.semaphore_signal(barrier, inc=1, device_id=device, device_id_type=MESH)
+    def chip_peer(step):
+        return lax.rem(chip + step, 8) * 2 + core, exp
+
+    def greet_chip(step, carry):
+        pl.semaphore_signal(barrier, inc=1, device_id=chip_peer(step), device_id_type=MESH)
+        return carry
+
+    pairs[...] = jnp.zeros_like(pairs)
+    pl.semaphore_signal(barrier, inc=1, device_id=sibling, device_id_type=MESH)
+    lax.fori_loop(1, 8, greet_chip, 0)
     lax.fori_loop(1, exps, greet_exp, 0)
     loads = []
     for source, target in (
@@ -716,7 +729,7 @@
         load = pltpu.make_async_copy(source, target, local_sems.at[len(loads)])
         load.start()
         loads.append(load)
-    pl.semaphore_wait(barrier, 2 + Z - 1 + exps - 1)
+    pl.semaphore_wait(barrier, 1 + 7 + exps - 1)
 
     def remote(source, target, send, recv, device):
         return pltpu.make_async_remote_copy(
@@ -737,29 +750,60 @@
         started.append(copy)
         return copy
 
-    def send_pairs(place, device):
-        return begin(pairs.at[place], pairs.at[place], device)
+    def kv_copy(step):
+        return remote(
+            pairs.at[me], pairs.at[me], kv_send.at[step], kv_recv.at[step], chip_peer(step)
+        )
+
+    def kv_pass(step):
+        at = lax.rem(chip - step + 8, 8) * 2 + core
+        return remote(pairs.at[at], pairs.at[at], pass_send.at[step], pass_recv.at[step], sibling)
+
+    def kv_start(step, carry):
+        @pl.when(chip + step < 8)
+        def _():
+            kv_copy(step).start()
+
+        return carry
+
+    def kv_forward(step, carry):
+        @pl.when(chip - step >= 0)
+        def _():
+            kv_copy(step).wait_recv()
+            kv_pass(step).start()
+
+        return carry
+
+    def kv_arrive(step, carry):
+        @pl.when(chip - step >= 0)
+        def _():
+            kv_pass(step).wait_recv()
+
+        return carry
+
+    def kv_sent(step, carry):
+        @pl.when(chip + step < 8)
+        def _():
+            kv_copy(step).wait_send()
+
+        @pl.when(chip - step >= 0)
+        def _():
+            kv_pass(step).wait_send()
+
+        return carry
 
     loads[0].wait()
     loads[1].wait()
-    beside = seq_of(z, 1 - x_hi, core)
-    crossing = send_pairs(me, across)
-    rings = [(step, x_hi, send_pairs(me, z_peer(step))) for step in (1, 3, 2)]
-    handed = [send_pairs(me, sibling)]
-    crossing.wait_recv()
-    rings += [(step, 1 - x_hi, send_pairs(beside, z_peer(step))) for step in (1, 3, 2)]
-    handed.append(send_pairs(beside, sibling))
+    lax.fori_loop(1, 8, kv_start, 0)
+    kv_pass(0).start()
 
     half_depth = out_proj.shape[0] // 2
     tops = [pl.ds(0, half_depth), pl.ds(half_depth, half_depth)]
     w_across = [begin(out_proj.at[top, :], weights.at[mine, top, :], across) for top in tops]
     w_pair = begin(out_proj, weights.at[mine], sibling)
 
-    for step, side, copy in rings:
-        copy.wait_recv()
-        handed.append(send_pairs(seq_of(z - step + Z, side, core), sibling))
-    for copy in handed:
-        copy.wait_recv()
+    lax.fori_loop(1, 8, kv_forward, 0)
+    lax.fori_loop(0, 8, kv_arrive, 0)
     loads[2].wait()
 
     scaling = head_width ** (-0.5)
@@ -768,9 +812,19 @@
     )
 
     def att_copy(head, step):
-        at = attended.at[z, :, pl.ds(pl.multiple_of(head * head_width, 128), head_width)]
-        index = (step - 1) * heads + head
-        return remote(at, at, att_send.at[index], att_recv.at[index], z_peer(step))
+        span = pl.ds(pl.multiple_of(head * head_width, 128), head_width)
+        index = step * heads + head
+        return remote(
+            attended.at[0, :, span],
+            attended.at[Z - step, :, span],
+            att_send.at[index],
+            att_recv.at[index],
+            z_peer(step),
+        )
+
+    far = remote(
+        attended.at[0], attended.at[2], att_send.at[0], att_recv.at[0], z_peer(2)
+    )
 
     def one_head(head, carry):
         span = pl.ds(pl.multiple_of(head * head_width, 128), head_width)
@@ -782,71 +836,89 @@
         totals = jnp.sum(probs, axis=1, keepdims=True)
         all_values = pairs[:, :, head_width : 2 * head_width].reshape(length, head_width)
         summed = dot(probs.astype(bf16), all_values)
-        attended[z, :, span] = (summed / totals).astype(bf16)
-        for step in range(1, Z):
+        attended[0, :, span] = (summed / totals).astype(bf16)
+        for step in (1, 3):
             att_copy(head, step).start()
         return carry
 
     lax.fori_loop(0, heads, one_head, 0)
 
-    def att_arrive(head, carry):
-        for step in range(1, Z):
-            att_copy(head, step).wait_recv()
-        return carry
-
-    lax.fori_loop(0, heads, att_arrive, 0)
-
-    def part_copy(chunk, first, step):
-        to = lax.rem(exp + step, exps)
-        span = halves(chunk)
-        index = first * exps + step
+    far.start()
+
+    def halves(chunk):
+        return pl.ds(pl.multiple_of(chunk * 2 * columns, 128), 2 * columns)
+
+    chunks = (x_hi, 1 - x_hi)
+    order = [(0, 0), (1, 0), (3, 0), (0, 1), (1, 1), (3, 1), (2, 0), (2, 1)]
+
+    def part_copy(place, which, step):
+        span = halves(chunks[which])
+        index = (place * 2 + which) * exps + step
         return remote(
-            part_send.at[to, :, span],
-            part_recv.at[exp, :, span],
+            part_send.at[lax.rem(exp + step, exps), place, :, span],
+            part_recv.at[exp, place, :, span],
             part_send_sem.at[index],
             part_recv_sem.at[index],
             exp_peer(step),
         )
 
-    def halves(chunk):
-        return pl.ds(pl.multiple_of(chunk * 2 * columns, 128), 2 * columns)
-
-    def project(chunk, first):
+    def project(place, which):
         for piece in range(2):
-            block = chunk * 2 + piece
+            block = chunks[which] * 2 + piece
             at = pl.ds(pl.multiple_of(block * columns, 128), columns)
-            rows = attended[...].reshape(Z * seq_rows, heads * head_width)
-            value = dot(rows, weights[block]).astype(bf16)
-            for z_to in range(Z):
-                for exp_to in range(exps):
-                    start = z_to * seq_rows + exp_to * tokens
-                    part_send[exp_to, z_to * tokens : (z_to + 1) * tokens, at] = value[
-                        start : start + tokens
-                    ]
+            value = dot(attended[place], weights[block]).astype(bf16)
+            for exp_to in range(exps):
+                part_send[exp_to, place, :, at] = value[exp_to * tokens : (exp_to + 1) * tokens]
 
         def part_start(step, carry):
-            part_copy(chunk, first, step).start()
+            part_copy(place, which, step).start()
             return carry
 
         lax.fori_loop(1, exps, part_start, 0)
 
-    def total_of(chunk, first):
+    def proj_copy(place, which):
+        span = halves(chunks[which])
+        index = place * 2 + which
+        return remote(
+            proj_send.at[place, :, span],
+            proj.at[z, :, span],
+            proj_send_sem.at[index],
+            proj_recv_sem.at[index],
+            z_peer(place),
+        )
+
+    def total_of(place, which):
         def part_arrive(step, carry):
-            part_copy(chunk, first, step).wait_recv()
+            part_copy(place, which, step).wait_recv()
             return carry
 
         lax.fori_loop(1, exps, part_arrive, 0)
-        span = halves(chunk)
+        span = halves(chunks[which])
 
         def add(step, total):
-            return total + part_recv[lax.rem(exp + step, exps), :, span].astype(f32)
-
-        total = lax.fori_loop(1, exps, add, part_send[exp, :, span].astype(f32))
-        proj_send[:, :, span] = total.astype(bf16).reshape(Z, tokens, 2 * columns)
+            return total + part_recv[lax.rem(exp + step, exps), place, :, span].astype(f32)
+
+        total = lax.fori_loop(1, exps, add, part_send[exp, place, :, span].astype(f32))
+        if place == 0:
+            proj[z, :, span] = total.astype(bf16)
+        else:
+            proj_send[place, :, span] = total.astype(bf16)
+            proj_copy(place, which).start()
+
+    def rows_arrive(place):
+        def att_arrive(head, carry):
+            att_copy(head, Z - place).wait_recv()
+            return carry
+
+        lax.fori_loop(0, heads, att_arrive, 0)
 
     loads[3].wait()
     w_pair.wait_recv()
-    project(x_hi, 0)
+    project(0, 0)
+    rows_arrive(1)
+    project(1, 0)
+    rows_arrive(3)
+    project(3, 0)
     w_pass = []
     for index, top in enumerate(tops):
         w_across[index].wait_recv()
@@ -854,47 +926,44 @@
         w_pass.append(begin(at, at, sibling))
     for copy in w_pass:
         copy.wait_recv()
-    project(1 - x_hi, 1)
-    total_of(x_hi, 0)
-    total_of(1 - x_hi, 1)
+    project(0, 1)
+    project(1, 1)
+    project(3, 1)
+    far.wait_recv()
+    project(2, 0)
+    project(2, 1)
+    for place, which in order:
+        total_of(place, which)
     loads[4].wait()
-
-    def proj_copy(step):
-        return remote(
-            proj_send.at[lax.rem(z + step, Z)],
-            proj.at[z],
-            proj_send_sem.at[step],
-            proj_recv_sem.at[step],
-            z_peer(step),
-        )
-
-    for step in range(1, Z):
-        proj_copy(step).start()
-    proj[z] = proj_send[z]
-    for step in range(1, Z):
-        proj_copy(step).wait_recv()
+    for place, which in order:
+        if place > 0:
+            proj_copy(place, which).wait_recv()
     for place in range(Z):
         span = slice(place * 4 * columns, (place + 1) * 4 * columns)
         out[:, span] = (held_residual[:, span].astype(f32) + proj[place].astype(f32)).astype(bf16)
 
+    lax.fori_loop(1, 8, kv_sent, 0)
+    kv_pass(0).wait_send()
     for copy in started:
         copy.wait_send()
 
     def att_sent(head, carry):
-        for step in range(1, Z):
+        for step in (1, 3):
             att_copy(head, step).wait_send()
         return carry
 
     lax.fori_loop(0, heads, att_sent, 0)
-
-    def part_sent(step, carry):
-        part_copy(x_hi, 0, step).wait_send()
-        part_copy(1 - x_hi, 1, step).wait_send()
-        return carry
-
-    lax.fori_loop(1, exps, part_sent, 0)
-    for step in range(1, Z):
-        proj_copy(step).wait_send()
+    far.wait_send()
+
+    for place, which in order:
+
+        def part_sent(step, carry, place=place, which=which):
+            part_copy(place, which, step).wait_send()
+            return carry
+
+        lax.fori_loop(1, exps, part_sent, 0)
+        if place > 0:
+            proj_copy(place, which).wait_send()
 
 
 def attention_layer(queries, key_heads, value_heads, out_proj, residual):
@@ -917,18 +986,22 @@
             pltpu.VMEM((16, seq_rows, 2 * head_width), bf16),
             pltpu.VMEM((4,) + out_proj.shape, bf16),
             pltpu.VMEM((Z, seq_rows, heads * head_width), bf16),
-            pltpu.VMEM((exps, Z * tokens, 4 * columns), bf16),
-            pltpu.VMEM((exps, Z * tokens, 4 * columns), bf16),
+            pltpu.VMEM((exps, Z, tokens, 4 * columns), bf16),
+            pltpu.VMEM((exps, Z, tokens, 4 * columns), bf16),
             pltpu.VMEM((Z, tokens, 4 * columns), bf16),
             pltpu.VMEM((Z, tokens, 4 * columns), bf16),
-            dma((20,)),
-            dma((20,)),
-            dma((3 * heads,)),
-            dma((3 * heads,)),
-            dma((2 * exps,)),
-            dma((2 * exps,)),
-            dma((Z,)),
-            dma((Z,)),
+            dma((8,)),
+            dma((8,)),
+            dma((8,)),
+            dma((8,)),
+            dma((5,)),
+            dma((5,)),
+            dma((4 * heads,)),
+            dma((4 * heads,)),
+            dma((8 * exps,)),
+            dma((8 * exps,)),
+            dma((2 * Z,)),
+            dma((2 * Z,)),
             dma((5,)),
         ],
         compiler_params=pltpu.CompilerParams(

time: 154 us -> 148 us (0.961)
  Pallas kernels: 152 us -> 146 us
    pallas_call x1, Pallas kernels: 55.3 us -> 49.7 us  [attention_layer(): pl.pallas_call(functools.partial(attention_kernel, exps), out_shape=jax.S...]
where the time goes in v2:
time: 148 us
  Pallas kernels  146 us (99%)
  local copies, waits for them, and re-layouts  1.62 us (1%)
    pallas_call x1, Pallas kernels, expert_layer(): pl.pallas_call(functools.partial(expert_kernel, exps), out_shape=jax.Shap...  96.3 us
    pallas_call x1, Pallas kernels, attention_layer(): pl.pallas_call(functools.partial(attention_kernel, exps), out_shape=jax.S...  49.7 us

profile of v2, /device:TPU:1, one launch (start us, length us, event | category | flops | bytes accessed | tf_op | source)
XLA Modules:
  0.0 147.6 jit_solution(18174522432033248138)
XLA Ops:
  0.0 49.7 %shard_map.136.hidden = bf16[16,6144]{1,0:T(8,128)(2,1)} custom-call(bf16[128,768]{1,0:T(8,128)(2,1)} %queries.1, bf16[128,128]{1,0:T(8,128)(2,1)} %key_heads.1, bf16[128,128]{1,0:T(8,128)(2,1)} %value_heads.1, bf16[768,384]{1,0:T(8,128)(2,1)} %out_proj.1, bf16[16,6144]{1,0:T(8,128)(2,1)} %residual.1), custom_call_target="tpu_custom_call" | custom-call | tf_op jit(solution)/shard_map/pallas_call | solution.py:978
  49.7 96.3 %shard_map.137 = bf16[16,6144]{1,0:T(8,128)(2,1)} custom-call(bf16[16,6144]{1,0:T(8,128)(2,1)} %shard_map.136.hidden, f32[1,6144]{1,0:T(1,128)} %bitcast.13, s32[2,16]{1,0:T(2,128)} %bitcast.14, f32[2,16]{1,0:T(2,128)} %bitcast.15, s32[16,64]{1,0:T(8,128)} %mix.1, bf16[512,6144]{1,0:T(8,128)(2,1)} %bitcast.8, bf16[512,6144]{1,0:T(8,128)(2,1)} %bitcast.9, ...), custom_call_target="tpu_custom_call" | custom-call | tf_op jit(solution)/shard_map/pallas_call | solution.py:594
  146.0 1.6 %copy.16 = bf16[16,6144]{1,0:T(8,128)(2,1)} copy(bf16[16,6144]{1,0:T(8,128)(2,1)} %shard_map.137) | data formatting | bytes 393216

commit v3 on v2

--- a/solution.py
+++ b/solution.py
@@ -325,11 +325,11 @@
 
     land(0)
     ring_own(0)
+    cross_own(0)
     land(1)
     for index in range(1, PIECES):
         cross_own(index)
     ring_own(1)
-    cross_own(0)
     relay(0, 0)
     spread_crossed(1)
     spread_crossed(2)

time: 148 us -> 145 us (0.980)
  Pallas kernels: 146 us -> 143 us
    pallas_call x1, Pallas kernels: 96.3 us -> 93.4 us  [expert_layer(): pl.pallas_call(functools.partial(expert_kernel, exps), out_shape=jax.Shap...]
where the time goes in v3:
time: 145 us
  Pallas kernels  143 us (99%)
  local copies, waits for them, and re-layouts  1.62 us (1%)
    pallas_call x1, Pallas kernels, expert_layer(): pl.pallas_call(functools.partial(expert_kernel, exps), out_shape=jax.Shap...  93.4 us
    pallas_call x1, Pallas kernels, attention_layer(): pl.pallas_call(functools.partial(attention_kernel, exps), out_shape=jax.S...  49.7 us

profile of v3, /device:TPU:1, one launch (start us, length us, event | category | flops | bytes accessed | tf_op | source)
XLA Modules:
  0.0 144.7 jit_solution(14476326990868524118)
XLA Ops:
  0.0 49.7 %shard_map.136.hidden = bf16[16,6144]{1,0:T(8,128)(2,1)} custom-call(bf16[128,768]{1,0:T(8,128)(2,1)} %queries.1, bf16[128,128]{1,0:T(8,128)(2,1)} %key_heads.1, bf16[128,128]{1,0:T(8,128)(2,1)} %value_heads.1, bf16[768,384]{1,0:T(8,128)(2,1)} %out_proj.1, bf16[16,6144]{1,0:T(8,128)(2,1)} %residual.1), custom_call_target="tpu_custom_call" | custom-call | tf_op jit(solution)/shard_map/pallas_call | solution.py:978
  49.7 93.4 %shard_map.137 = bf16[16,6144]{1,0:T(8,128)(2,1)} custom-call(bf16[16,6144]{1,0:T(8,128)(2,1)} %shard_map.136.hidden, f32[1,6144]{1,0:T(1,128)} %bitcast.13, s32[2,16]{1,0:T(2,128)} %bitcast.14, f32[2,16]{1,0:T(2,128)} %bitcast.15, s32[16,64]{1,0:T(8,128)} %mix.1, bf16[512,6144]{1,0:T(8,128)(2,1)} %bitcast.8, bf16[512,6144]{1,0:T(8,128)(2,1)} %bitcast.9, ...), custom_call_target="tpu_custom_call" | custom-call | tf_op jit(solution)/shard_map/pallas_call | solution.py:594
  143.1 1.6 %copy.16 = bf16[16,6144]{1,0:T(8,128)(2,1)} copy(bf16[16,6144]{1,0:T(8,128)(2,1)} %shard_map.137) | data formatting | bytes 393216
